TPU v7x, 512 devices: a whole 4x8x8 slice. The times are simulated.
512 devices in a mesh: tm: 128 (over z_lo, x, y, core), series: 4 (over z_hi).
Axes of the slice: x: 4, y: 8, z: 8 (z_hi: 4, z_lo: 2; z = z_hi * 2 + z_lo), core: 2. Of those that a mesh axis runs over, the one named last changes fastest.
Arguments:
- time_query: bfloat16 [20, 8192, 512], P('series', 'tm'), may hold values from -160 to 160
- time_key: bfloat16 [20, 8192, 512], P('series', 'tm'), may hold values from -6 to 6
- time_value: bfloat16 [20, 8192, 512], P('series', 'tm'), may hold values from -6 to 6
- group_query: bfloat16 [20, 8192, 512], P('series', 'tm'), may hold values from -160 to 160
- group_key: bfloat16 [20, 8192, 512], P('series', 'tm'), may hold values from -6 to 6
- group_value: bfloat16 [20, 8192, 512], P('series', 'tm'), may hold values from -6 to 6
- out_time: bfloat16 [512, 768], P('series'), may hold values from -0.25 to 0.25
- out_group: bfloat16 [512, 768], P('series'), may hold values from -0.25 to 0.25
- series_group: int32 [20], replicated, may hold values from 0 to 1, as said below
- band_width: int32 [8], replicated, may hold values from 2 to 16, as said below
- cotangent: bfloat16 [20, 8192, 768], P('series', 'tm'), may hold values from -6 to 6
Outputs:
- grad_time_query: bfloat16 [20, 8192, 512], P('series', 'tm')
- grad_time_key: bfloat16 [20, 8192, 512], P('series', 'tm')
- grad_time_value: bfloat16 [20, 8192, 512], P('series', 'tm')
- grad_group_query: bfloat16 [20, 8192, 512], P('series', 'tm')
- grad_group_key: bfloat16 [20, 8192, 512], P('series', 'tm')
- grad_group_value: bfloat16 [20, 8192, 512], P('series', 'tm')
- grad_out_time: float32 [512, 768], P('series', 'tm')
- grad_out_group: float32 [512, 768], P('series', 'tm')
Inputs may be any that keep to these rules, and one draw needn't show every extreme that they name: `series_group`: series with equal numbers form one group; there are two groups, one of exactly 16 series and one of exactly 4. `band_width`: some head's band is exactly 16.
All inputs are finite; a program needn't handle non-finite values.
Results may differ from a plain program's by a relative error of at most 0.0058.
Values may be sent and summed in bfloat16 or wider, within the bound.
No kernel may reach another device: no remote copies, remote signals or barrier semaphores. Data moves between devices by JAX's collectives and lax.ppermute only.
A program may use at most 128 MiB of HBM per device.

v0:
```python
import jax
import jax.numpy as jnp
from jax import lax
from jax.sharding import PartitionSpec as P

HEAD_DIM = 64
BAND = 16
masked_score = -1e30


def passed_along(value, axis, steps):
    count = lax.axis_size(axis)
    leading, last = (max(0, -steps), min(count, count - steps))
    return lax.ppermute(value, axis, [(source, source + steps) for source in range(leading, last)])


def soft_weights(scores, keep_mask):
    scores = jnp.where(keep_mask, scores, masked_score)
    row_top = jnp.max(scores, axis=-1, keepdims=True)
    weights = jnp.exp(scores - row_top)
    return weights / jnp.sum(weights, axis=-1, keepdims=True)


def score_grad(probabilities, grad_prob, score_scale):
    grad_inner = lax.optimization_barrier(grad_prob.astype(jnp.bfloat16)).astype(jnp.float32)
    centred = grad_inner - jnp.sum(grad_inner * probabilities, axis=-1, keepdims=True)
    return probabilities * centred * score_scale


def temporal_attend(query_rows, key_ext, value_ext, out_grad, band_width, first_row):
    ser_count, block_rows, row_width = query_rows.shape
    head_count = band_width.shape[0]
    head_depth = row_width // head_count
    border_rows = key_ext.shape[1] - block_rows
    score_scale = head_depth ** (-0.5)
    query_heads = query_rows.reshape(ser_count, block_rows, head_count, head_depth)
    key_heads = key_ext.reshape(ser_count, block_rows + border_rows, head_count, head_depth)
    value_heads = value_ext.reshape(ser_count, block_rows + border_rows, head_count, head_depth)
    grad_heads = out_grad.reshape(ser_count, block_rows, head_count, head_depth)
    scores = (
        jnp.einsum("sthd,sihd->shti", query_heads, key_heads, preferred_element_type=jnp.float32)
        * score_scale
    )
    query_pos = lax.broadcasted_iota(jnp.int32, (block_rows, block_rows + border_rows), 0)
    key_pos = lax.broadcasted_iota(jnp.int32, (block_rows, block_rows + border_rows), 1)
    offset = query_pos + border_rows - key_pos
    absolute = first_row + key_pos - border_rows
    in_band = (
        (offset[None] >= 0) & (offset[None] < band_width[:, None, None]) & (absolute[None] >= 0)
    )
    probabilities = soft_weights(scores, in_band[None])
    rounded = probabilities.astype(jnp.bfloat16)
    mixed_out = jnp.einsum(
        "shti,sihd->sthd", rounded, value_heads, preferred_element_type=jnp.float32
    )
    grad_value = jnp.einsum(
        "shti,sthd->sihd", rounded, grad_heads, preferred_element_type=jnp.float32
    )
    grad_prob = jnp.einsum(
        "sthd,sihd->shti", grad_heads, value_heads, preferred_element_type=jnp.float32
    )
    grad_score = score_grad(probabilities, grad_prob, score_scale)
    grad_query = jnp.einsum(
        "shti,sihd->sthd",
        grad_score,
        key_heads.astype(jnp.float32),
        precision=lax.Precision.HIGHEST,
    )
    grad_key = jnp.einsum(
        "shti,sthd->sihd",
        grad_score,
        query_heads.astype(jnp.float32),
        precision=lax.Precision.HIGHEST,
    )
    ext_rows = block_rows + border_rows
    return (
        mixed_out.reshape(ser_count, block_rows, row_width),
        grad_query.reshape(ser_count, block_rows, row_width),
        grad_key.reshape(ser_count, ext_rows, row_width),
        grad_value.reshape(ser_count, ext_rows, row_width),
    )


def group_attend(query_rows, key_rows, value_rows, out_grad, series_group):
    ser_count, block_rows, row_width = query_rows.shape
    head_count = row_width // HEAD_DIM
    score_scale = HEAD_DIM ** (-0.5)
    query_heads = query_rows.reshape(ser_count, block_rows, head_count, HEAD_DIM)
    key_heads = key_rows.reshape(ser_count, block_rows, head_count, HEAD_DIM)
    value_heads = value_rows.reshape(ser_count, block_rows, head_count, HEAD_DIM)
    grad_heads = out_grad.reshape(ser_count, block_rows, head_count, HEAD_DIM)
    scores = (
        jnp.einsum("sthd,rthd->thsr", query_heads, key_heads, preferred_element_type=jnp.float32)
        * score_scale
    )
    same_group = series_group[:, None] == series_group[None, :]
    probabilities = soft_weights(scores, same_group[None, None])
    rounded = probabilities.astype(jnp.bfloat16)
    mixed_out = jnp.einsum(
        "thsr,rthd->sthd", rounded, value_heads, preferred_element_type=jnp.float32
    )
    grad_value = jnp.einsum(
        "thsr,sthd->rthd", rounded, grad_heads, preferred_element_type=jnp.float32
    )
    grad_prob = jnp.einsum(
        "sthd,rthd->thsr", grad_heads, value_heads, preferred_element_type=jnp.float32
    )
    grad_score = score_grad(probabilities, grad_prob, score_scale)
    grad_query = jnp.einsum(
        "thsr,rthd->sthd",
        grad_score,
        key_heads.astype(jnp.float32),
        precision=lax.Precision.HIGHEST,
    )
    grad_key = jnp.einsum(
        "thsr,sthd->rthd",
        grad_score,
        query_heads.astype(jnp.float32),
        precision=lax.Precision.HIGHEST,
    )
    out_shape = (ser_count, block_rows, row_width)
    return (
        mixed_out.reshape(out_shape),
        grad_query.reshape(out_shape),
        grad_key.reshape(out_shape),
        grad_value.reshape(out_shape),
    )


def group_local(moved_parts, series_group):
    query_rows, key_rows, value_rows, out_grad = moved_parts
    mixed_out, grad_query, grad_key, grad_value = group_attend(
        query_rows, key_rows, value_rows, out_grad, series_group
    )
    return (
        mixed_out.astype(jnp.bfloat16),
        grad_query.astype(jnp.bfloat16),
        grad_key.astype(jnp.bfloat16),
        grad_value.astype(jnp.bfloat16),
    )


def per_device(
    time_query,
    time_key,
    time_value,
    group_query,
    group_key,
    group_value,
    out_time,
    out_group,
    series_group,
    band_width,
    cotangent,
):
    ser_dev, block_rows, row_width = time_query.shape
    border_rows = BAND - 1
    w_time, w_group = (
        lax.all_gather(out_time, "series", axis=0, tiled=True),
        lax.all_gather(out_group, "series", axis=0, tiled=True),
    )
    cot_flat = cotangent.reshape(-1, cotangent.shape[2])

    def back_project(weight):
        product = lax.dot_general(
            cot_flat, weight, (((1,), (1,)), ((), ())), preferred_element_type=jnp.float32
        )
        return product.astype(jnp.bfloat16).reshape(ser_dev, block_rows, row_width)

    d_time = back_project(w_time)
    d_group = back_project(w_group)
    rim_key, rim_value = passed_along(
        (time_key[:, block_rows - border_rows :], time_value[:, block_rows - border_rows :]),
        "tm",
        1,
    )
    key_ext = jnp.concatenate([rim_key, time_key], axis=1)
    value_ext = jnp.concatenate([rim_value, time_value], axis=1)
    first_row = lax.axis_index("tm") * block_rows
    temporal_mixture, temporal_query_gradient, extended_key_gradient, extended_value_gradient = (
        temporal_attend(time_query, key_ext, value_ext, d_time, band_width, first_row)
    )
    time_out = temporal_mixture.astype(jnp.bfloat16)
    pulled_key_rows, pulled_value_rows = passed_along(
        (extended_key_gradient[:, :border_rows], extended_value_gradient[:, :border_rows]), "tm", -1
    )
    empty_padding_rows = jnp.zeros((ser_dev, block_rows - border_rows, row_width), jnp.float32)
    grad_tk = (
        extended_key_gradient[:, border_rows:]
        + jnp.concatenate([empty_padding_rows, pulled_key_rows], axis=1)
    ).astype(jnp.bfloat16)
    temporal_value_gradient = (
        extended_value_gradient[:, border_rows:]
        + jnp.concatenate([empty_padding_rows, pulled_value_rows], axis=1)
    ).astype(jnp.bfloat16)
    temporal_query_gradient = temporal_query_gradient.astype(jnp.bfloat16)
    moved_parts = (
        lax.all_to_all(group_query, "series", split_axis=1, concat_axis=0, tiled=True),
        lax.all_to_all(group_key, "series", split_axis=1, concat_axis=0, tiled=True),
        lax.all_to_all(group_value, "series", split_axis=1, concat_axis=0, tiled=True),
        lax.all_to_all(d_group, "series", split_axis=1, concat_axis=0, tiled=True),
    )
    results = group_local(moved_parts, series_group)
    group_out, grad_gq, grad_gk, grad_gv = (
        lax.all_to_all(results[0], "series", split_axis=0, concat_axis=1, tiled=True),
        lax.all_to_all(results[1], "series", split_axis=0, concat_axis=1, tiled=True),
        lax.all_to_all(results[2], "series", split_axis=0, concat_axis=1, tiled=True),
        lax.all_to_all(results[3], "series", split_axis=0, concat_axis=1, tiled=True),
    )
    grad_scale = (ser_dev * block_rows * lax.axis_size("series") * lax.axis_size("tm")) ** (-0.5)
    term_time = (
        lax.dot_general(
            time_out.reshape(-1, row_width),
            cot_flat,
            (((0,), (0,)), ((), ())),
            preferred_element_type=jnp.float32,
        )
        * grad_scale
    )
    term_group = (
        lax.dot_general(
            group_out.reshape(-1, row_width),
            cot_flat,
            (((0,), (0,)), ((), ())),
            preferred_element_type=jnp.float32,
        )
        * grad_scale
    )
    partial_sums = (
        lax.psum_scatter(term_time, "tm", scatter_dimension=1, tiled=True),
        lax.psum_scatter(term_group, "tm", scatter_dimension=1, tiled=True),
    )
    grad_wt, grad_wg = (
        lax.psum_scatter(partial_sums[0], "series", scatter_dimension=0, tiled=True),
        lax.psum_scatter(partial_sums[1], "series", scatter_dimension=0, tiled=True),
    )
    return (
        temporal_query_gradient,
        grad_tk,
        temporal_value_gradient,
        grad_gq,
        grad_gk,
        grad_gv,
        grad_wt,
        grad_wg,
    )


def solution(mesh):
    placed = (
        P("series", "tm", None),
        P("series", "tm", None),
        P("series", "tm", None),
        P("series", "tm", None),
        P("series", "tm", None),
        P("series", "tm", None),
        P("series", None),
        P("series", None),
        P(),
        P(),
        P("series", "tm", None),
    )
    return jax.shard_map(
        per_device,
        mesh=mesh,
        in_specs=placed,
        out_specs=(
            P("series", "tm", None),
            P("series", "tm", None),
            P("series", "tm", None),
            P("series", "tm", None),
            P("series", "tm", None),
            P("series", "tm", None),
            P("series", "tm"),
            P("series", "tm"),
        ),
        check_vma=False,
    )
```

profile of v0, /device:TPU:2, one launch (start us, length us, event | category | flops | bytes accessed | tf_op | source)
XLA Modules:
  0.0 800.1 jit_solution(5145301826097418971)
XLA Ops:
  11.1 19.1 %collective-permute-start.1 = (bf16[5,15,512]{2,1,0:T(8,128)(2,1)S(1)}, bf16[5,15,512]{2,1,0:T(8,128)(2,1)S(1)}, u32[]{:S(2)}, u32[]{:S(2)}) collective-permute-start(bf16[5,15,512]{2,1,0:T(8,128)(2,1)S(1)} %slice.19), channel_id=1, source_target_pairs={{0,4},{4,8},{8,12},{12,16},{16,20},{20,24},{24,28},{28,32},{32,36}... | collective-permute-start | bytes 230408 | tf_op jit(solution)/shard_map/ppermute | solution.py:14
  32.1 8.7 %all-to-all-start.3 = ((bf16[5,64,512]{2,0,1:T(8,128)(2,1)}), bf16[5,64,512]{2,0,1:T(8,128)(2,1)}, u32[]{:S(2)}, u32[]{:S(2)}) async-start(bf16[5,64,512]{2,0,1:T(8,128)(2,1)} %copy.160), calls=%async_computation.3 | async-start | bytes 1048576 | tf_op jit(solution)/shard_map/all_to_all | solution.py:200
  41.0 30.3 %all_gather.6 = bf16[512,768]{1,0:T(8,128)(2,1)S(1)} all-gather(bf16[128,768]{1,0:T(8,128)(2,1)S(1)} %copy-done.27), channel_id=1, replica_groups=mesh['tm'=128,'series'=4] {'series'}, dimensions={0}, use_global_device_ids=true | all-gather | bytes 983040 | tf_op jit(solution)/shard_map/all_gather | solution.py:159
  71.3 17.7 %all_gather.7 = bf16[512,768]{1,0:T(8,128)(2,1)S(1)} all-gather(bf16[128,768]{1,0:T(8,128)(2,1)S(1)} %copy-done.28), channel_id=1, replica_groups=mesh['tm'=128,'series'=4] {'series'}, dimensions={0}, use_global_device_ids=true | all-gather | bytes 983040 | tf_op jit(solution)/shard_map/all_gather | solution.py:160
  96.9 5.6 all-to-all-start.1
  104.0 6.9 fusion.53
  110.9 4.6 all-to-all-done.1
  115.5 4.1 all-to-all-start
  143.1 5.7 all-to-all-start.7
  148.7 7.3 convolution_convert_fusion.5
  161.5 4.8 all-to-all-start.2
  168.1 269.2 %fusion.52 = (f32[512,8]{0,1:T(8,128)S(1)}, f32[512,8]{0,1:T(8,128)S(1)}) fusion(f32[512,768]{0,1:T(8,128)} %bitcast_multiply_fusion, f32[512,768]{0,1:T(8,128)} %convolution_multiply_fusion), kind=kCustom, calls=%all-reduce-scatter.2 | all-reduce-scatter fusion | flops 1048577 | bytes 3180544
  438.6 12.3 %collective-permute-start.33 = (f32[512,8]{0,1:T(8,128)S(1)}, f32[512,8]{0,1:T(8,128)S(1)}, u32[]{:S(2)}, u32[]{:S(2)}) collective-permute-start(f32[512,8]{0,1:T(8,128)S(1)} %get-tuple-element.50), channel_id=1, source_target_pairs={{0,120},{4,124},{8,128},{12,132},{16,136},{20,140},{24,144},{28,14... | collective-permute-start | bytes 49160
  450.9 7.8 collective-permute-start.32
  461.5 18.1 %collective-permute-start.31 = (f32[512,8]{0,1:T(8,128)S(1)}, f32[512,8]{0,1:T(8,128)S(1)}, u32[]{:S(2)}, u32[]{:S(2)}) collective-permute-start(f32[512,8]{0,1:T(8,128)S(1)} %get-tuple-element.50), channel_id=1, source_target_pairs={{0,112},{4,116},{8,120},{12,124},{16,128},{20,132},{24,136},{28,14... | collective-permute-start | bytes 49160
  479.6 10.9 %collective-permute-start.30 = (f32[512,8]{0,1:T(8,128)S(1)}, f32[512,8]{0,1:T(8,128)S(1)}, u32[]{:S(2)}, u32[]{:S(2)}) collective-permute-start(f32[512,8]{0,1:T(8,128)S(1)} %get-tuple-element.50), channel_id=1, source_target_pairs={{0,108},{4,112},{8,116},{12,120},{16,124},{20,128},{24,132},{28,13... | collective-permute-start | bytes 49160
  490.6 17.6 %collective-permute-start.29 = (f32[512,8]{0,1:T(8,128)S(1)}, f32[512,8]{0,1:T(8,128)S(1)}, u32[]{:S(2)}, u32[]{:S(2)}) collective-permute-start(f32[512,8]{0,1:T(8,128)S(1)} %get-tuple-element.50), channel_id=1, source_target_pairs={{0,104},{4,108},{8,112},{12,116},{16,120},{20,124},{24,128},{28,13... | collective-permute-start | bytes 49160
  519.2 4.5 collective-permute-start.22
  550.0 4.1 collective-permute-start.12
  555.1 4.2 collective-permute-start.11
  561.3 4.0 collective-permute-start.9
  571.6 14.8 %fusion.10 = f32[16,8,20,20]{3,1,2,0:T(8,128)} fusion(bf16[16,8,20,20]{3,1,2,0:T(8,128)(2,1)S(1)} %copy.214, f32[16,8,20,20]{3,1,2,0:T(8,128)S(1)} %copy-done.9, f32[16,8,20]{1,2,0:T(8,128)S(1)} %copy-done.21), kind=kOutput, calls=%fused_computation.14 | output fusion | flops 412179 | bytes 522240 | tf_op jit(solution)/shard_map/sub | solution.py:26
  605.0 5.0 all-to-all-start.4
  619.6 4.2 convolution_convert_fusion.4
  637.2 7.1 all-to-all-start.5
  655.0 7.3 fusion.45
  687.5 7.1 all-to-all-start.6
  711.2 8.1 %concatenate.16 = f32[512,262]{0,1:T(8,128)S(1)} concatenate(f32[512,6]{0,1:T(8,128)S(1)} %copy-done.41, f32[512,8]{0,1:T(8,128)S(1)} %copy-done.35, f32[512,8]{0,1:T(8,128)S(1)} %copy-done.37, f32[512,8]{0,1:T(8,128)S(1)} %copy-done.39, f32[512,8]{0,1:T(8,128)S(1)} %copy-done.43, f32[512,8]{0,1:T(8,128)S(1)} %copy-done.45, f32[512,8]{0,1:T(8,128)S(1)} %copy-done.47, ...), dimensions={1} | concatenate | bytes 1073152
  719.4 6.1 collective-permute-start.3
  739.1 9.6 %concatenate.17 = f32[512,262]{0,1:T(8,128)S(1)} concatenate(f32[512,6]{0,1:T(8,128)S(1)} %copy-done.33, f32[512,8]{0,1:T(8,128)S(1)} %copy-done.73, f32[512,8]{0,1:T(8,128)S(1)} %copy-done.75, f32[512,8]{0,1:T(8,128)S(1)} %copy-done.83, f32[512,8]{0,1:T(8,128)S(1)} %copy-done.87, f32[512,8]{0,1:T(8,128)S(1)} %copy-done.91, f32[512,8]{0,1:T(8,128)S(1)} %copy-done.93, ...), dimensions={1} | concatenate | bytes 1073152
  753.3 10.1 %reduce-scatter.7.cloned.1.call-done = f32[128,6]{0,1:T(8,128)} async-done(((f32[512,6]{0,1:T(8,128)}), f32[128,6]{0,1:T(8,128)}) %reduce-scatter.7.cloned.1.call-update) | async-done | bytes 3088 | tf_op jit(solution)/shard_map/reduce_scatter | solution.py:234
  763.4 29.6 %reduce-scatter.9.cloned.1.call-done = f32[128,6]{0,1:T(8,128)} async-done(((f32[512,6]{0,1:T(8,128)}), f32[128,6]{0,1:T(8,128)}) %reduce-scatter.9.cloned.1.call-update) | async-done | bytes 3088 | tf_op jit(solution)/shard_map/reduce_scatter | solution.py:235
  (416 shorter events, 206.0 us)
Async XLA Ops:
  8.2 86.9 %collective-permute-start = (bf16[5,15,512]{2,1,0:T(8,128)(2,1)S(1)}, bf16[5,15,512]{2,1,0:T(8,128)(2,1)S(1)}, u32[]{:S(2)}, u32[]{:S(2)}) collective-permute-start(bf16[5,15,512]{2,1,0:T(8,128)(2,1)S(1)} %slice.18), channel_id=1, source_target_pairs={{0,4},{4,8},{8,12},{12,16},{16,20},{20,24},{24,28},{28,32},{32,36}... | collective-permute-start | bytes 230408 | tf_op jit(solution)/shard_map/ppermute | solution.py:14
  11.1 84.5 %collective-permute-start.1 = (bf16[5,15,512]{2,1,0:T(8,128)(2,1)S(1)}, bf16[5,15,512]{2,1,0:T(8,128)(2,1)S(1)}, u32[]{:S(2)}, u32[]{:S(2)}) collective-permute-start(bf16[5,15,512]{2,1,0:T(8,128)(2,1)S(1)} %slice.19), channel_id=1, source_target_pairs={{0,4},{4,8},{8,12},{12,16},{16,20},{20,24},{24,28},{28,32},{32,36}... | collective-permute-start | bytes 230408 | tf_op jit(solution)/shard_map/ppermute | solution.py:14
  32.1 64.3 %all-to-all-start.3 = ((bf16[5,64,512]{2,0,1:T(8,128)(2,1)}), bf16[5,64,512]{2,0,1:T(8,128)(2,1)}, u32[]{:S(2)}, u32[]{:S(2)}) async-start(bf16[5,64,512]{2,0,1:T(8,128)(2,1)} %copy.160), calls=%async_computation.3 | async-start | bytes 1048576 | tf_op jit(solution)/shard_map/all_to_all | solution.py:200
  124.2 335.9 %collective-permute-start.2 = (f32[5,15,512]{2,1,0:T(8,128)}, f32[5,15,512]{2,1,0:T(8,128)S(1)}, u32[]{:S(2)}, u32[]{:S(2)}) collective-permute-start(f32[5,15,512]{2,1,0:T(8,128)} %copy.186), channel_id=1, source_target_pairs={{4,0},{8,4},{12,8},{16,12},{20,16},{24,20},{28,24},{32,28},{36,32}... | collective-permute-start | bytes 460808 | tf_op jit(solution)/shard_map/ppermute | solution.py:14
  161.5 377.2 %all-to-all-start.2 = ((bf16[5,64,512]{2,0,1:T(8,128)(2,1)}), bf16[5,64,512]{2,0,1:T(8,128)(2,1)S(1)}, u32[]{:S(2)}, u32[]{:S(2)}) async-start(bf16[5,64,512]{2,0,1:T(8,128)(2,1)} %copy.157), calls=%async_computation.2 | async-start | bytes 1048576 | tf_op jit(solution)/shard_map/all_to_all | solution.py:201
  437.3 53.3 %collective-permute-start.34 = (f32[512,8]{0,1:T(8,128)S(1)}, f32[512,8]{0,1:T(8,128)S(1)}, u32[]{:S(2)}, u32[]{:S(2)}) collective-permute-start(f32[512,8]{0,1:T(8,128)S(1)} %get-tuple-element.50), channel_id=1, source_target_pairs={{0,124},{4,128},{8,132},{12,136},{16,140},{20,144},{24,148},{28,15... | collective-permute-start | bytes 49160
  438.6 69.6 %collective-permute-start.33 = (f32[512,8]{0,1:T(8,128)S(1)}, f32[512,8]{0,1:T(8,128)S(1)}, u32[]{:S(2)}, u32[]{:S(2)}) collective-permute-start(f32[512,8]{0,1:T(8,128)S(1)} %get-tuple-element.50), channel_id=1, source_target_pairs={{0,120},{4,124},{8,128},{12,132},{16,136},{20,140},{24,144},{28,14... | collective-permute-start | bytes 49160
  450.9 59.2 %collective-permute-start.32 = (f32[512,8]{0,1:T(8,128)S(1)}, f32[512,8]{0,1:T(8,128)S(1)}, u32[]{:S(2)}, u32[]{:S(2)}) collective-permute-start(f32[512,8]{0,1:T(8,128)S(1)} %get-tuple-element.50), channel_id=1, source_target_pairs={{0,116},{4,120},{8,124},{12,128},{16,132},{20,136},{24,140},{28,14... | collective-permute-start | bytes 49160
  461.5 51.7 %collective-permute-start.31 = (f32[512,8]{0,1:T(8,128)S(1)}, f32[512,8]{0,1:T(8,128)S(1)}, u32[]{:S(2)}, u32[]{:S(2)}) collective-permute-start(f32[512,8]{0,1:T(8,128)S(1)} %get-tuple-element.50), channel_id=1, source_target_pairs={{0,112},{4,116},{8,120},{12,124},{16,128},{20,132},{24,136},{28,14... | collective-permute-start | bytes 49160
  479.6 35.0 %collective-permute-start.30 = (f32[512,8]{0,1:T(8,128)S(1)}, f32[512,8]{0,1:T(8,128)S(1)}, u32[]{:S(2)}, u32[]{:S(2)}) collective-permute-start(f32[512,8]{0,1:T(8,128)S(1)} %get-tuple-element.50), channel_id=1, source_target_pairs={{0,108},{4,112},{8,116},{12,120},{16,124},{20,128},{24,132},{28,13... | collective-permute-start | bytes 49160
  490.6 25.3 %collective-permute-start.29 = (f32[512,8]{0,1:T(8,128)S(1)}, f32[512,8]{0,1:T(8,128)S(1)}, u32[]{:S(2)}, u32[]{:S(2)}) collective-permute-start(f32[512,8]{0,1:T(8,128)S(1)} %get-tuple-element.50), channel_id=1, source_target_pairs={{0,104},{4,108},{8,112},{12,116},{16,120},{20,124},{24,128},{28,13... | collective-permute-start | bytes 49160
  555.1 33.6 %collective-permute-start.11 = (f32[512,8]{0,1:T(8,128)S(1)}, f32[512,8]{0,1:T(8,128)S(1)}, u32[]{:S(2)}, u32[]{:S(2)}) collective-permute-start(f32[512,8]{0,1:T(8,128)S(1)} %get-tuple-element.50), channel_id=1, source_target_pairs={{0,32},{4,36},{8,40},{12,44},{16,48},{20,52},{24,56},{28,60},{32,6... | collective-permute-start | bytes 49160
  559.4 32.7 %collective-permute-start.10 = (f32[512,8]{0,1:T(8,128)S(1)}, f32[512,8]{0,1:T(8,128)S(1)}, u32[]{:S(2)}, u32[]{:S(2)}) collective-permute-start(f32[512,8]{0,1:T(8,128)S(1)} %get-tuple-element.50), channel_id=1, source_target_pairs={{0,28},{4,32},{8,36},{12,40},{16,44},{20,48},{24,52},{28,56},{32,6... | collective-permute-start | bytes 49160
  561.3 32.7 %collective-permute-start.9 = (f32[512,8]{0,1:T(8,128)S(1)}, f32[512,8]{0,1:T(8,128)S(1)}, u32[]{:S(2)}, u32[]{:S(2)}) collective-permute-start(f32[512,8]{0,1:T(8,128)S(1)} %get-tuple-element.50), channel_id=1, source_target_pairs={{0,24},{4,28},{8,32},{12,36},{16,40},{20,44},{24,48},{28,52},{32,5... | collective-permute-start | bytes 49160
  565.4 30.9 %collective-permute-start.8 = (f32[512,8]{0,1:T(8,128)S(1)}, f32[512,8]{0,1:T(8,128)S(1)}, u32[]{:S(2)}, u32[]{:S(2)}) collective-permute-start(f32[512,8]{0,1:T(8,128)S(1)} %get-tuple-element.50), channel_id=1, source_target_pairs={{0,20},{4,24},{8,28},{12,32},{16,36},{20,40},{24,44},{28,48},{32,5... | collective-permute-start | bytes 49160
  569.2 28.4 %collective-permute-start.7 = (f32[512,8]{0,1:T(8,128)S(1)}, f32[512,8]{0,1:T(8,128)S(1)}, u32[]{:S(2)}, u32[]{:S(2)}) collective-permute-start(f32[512,8]{0,1:T(8,128)S(1)} %get-tuple-element.50), channel_id=1, source_target_pairs={{0,16},{4,20},{8,24},{12,28},{16,32},{20,36},{24,40},{28,44},{32,4... | collective-permute-start | bytes 49160
  605.0 32.1 %all-to-all-start.4 = ((bf16[20,16,512]{2,1,0:T(8,128)(2,1)}), bf16[20,16,512]{2,1,0:T(8,128)(2,1)}, u32[]{:S(2)}, u32[]{:S(2)}) async-start(bf16[20,16,512]{2,1,0:T(8,128)(2,1)} %convert_element_type.102), calls=%async_computation.4 | async-start | bytes 655360 | tf_op jit(solution)/shard_map/all_to_all | solution.py:206
  637.2 50.3 %all-to-all-start.5 = ((bf16[20,16,512]{2,1,0:T(8,128)(2,1)}), bf16[20,16,512]{2,1,0:T(8,128)(2,1)S(1)}, u32[]{:S(2)}, u32[]{:S(2)}) async-start(bf16[20,16,512]{2,1,0:T(8,128)(2,1)} %convert_element_type.105), calls=%async_computation.5 | async-start | bytes 655360 | tf_op jit(solution)/shard_map/all_to_all | solution.py:207
  644.3 29.3 %collective-permute-start.54 = (f32[512,8]{0,1:T(8,128)S(1)}, f32[512,8]{0,1:T(8,128)S(1)}, u32[]{:S(2)}, u32[]{:S(2)}) collective-permute-start(f32[512,8]{0,1:T(8,128)S(1)} %get-tuple-element.51), channel_id=1, source_target_pairs={{0,76},{4,80},{8,84},{12,88},{16,92},{20,96},{24,100},{28,104},{32... | collective-permute-start | bytes 49160
  645.7 29.8 %collective-permute-start.53 = (f32[512,8]{0,1:T(8,128)S(1)}, f32[512,8]{0,1:T(8,128)S(1)}, u32[]{:S(2)}, u32[]{:S(2)}) collective-permute-start(f32[512,8]{0,1:T(8,128)S(1)} %get-tuple-element.51), channel_id=1, source_target_pairs={{0,72},{4,76},{8,80},{12,84},{16,88},{20,92},{24,96},{28,100},{32,... | collective-permute-start | bytes 49160
  648.0 29.5 %collective-permute-start.52 = (f32[512,8]{0,1:T(8,128)S(1)}, f32[512,8]{0,1:T(8,128)}, u32[]{:S(2)}, u32[]{:S(2)}) collective-permute-start(f32[512,8]{0,1:T(8,128)S(1)} %get-tuple-element.51), channel_id=1, source_target_pairs={{0,68},{4,72},{8,76},{12,80},{16,84},{20,88},{24,92},{28,96},{32,1... | collective-permute-start | bytes 49160
  649.9 29.9 %collective-permute-start.51 = (f32[512,8]{0,1:T(8,128)S(1)}, f32[512,8]{0,1:T(8,128)}, u32[]{:S(2)}, u32[]{:S(2)}) collective-permute-start(f32[512,8]{0,1:T(8,128)S(1)} %get-tuple-element.51), channel_id=1, source_target_pairs={{0,64},{4,68},{8,72},{12,76},{16,80},{20,84},{24,88},{28,92},{32,9... | collective-permute-start | bytes 49160
  652.0 30.0 %collective-permute-start.50 = (f32[512,8]{0,1:T(8,128)S(1)}, f32[512,8]{0,1:T(8,128)}, u32[]{:S(2)}, u32[]{:S(2)}) collective-permute-start(f32[512,8]{0,1:T(8,128)S(1)} %get-tuple-element.51), channel_id=1, source_target_pairs={{0,60},{4,64},{8,68},{12,72},{16,76},{20,80},{24,84},{28,88},{32,9... | collective-permute-start | bytes 49160
  682.0 24.8 %collective-permute-start.45 = (f32[512,8]{0,1:T(8,128)S(1)}, f32[512,8]{0,1:T(8,128)S(1)}, u32[]{:S(2)}, u32[]{:S(2)}) collective-permute-start(f32[512,8]{0,1:T(8,128)S(1)} %get-tuple-element.51), channel_id=1, source_target_pairs={{0,40},{4,44},{8,48},{12,52},{16,56},{20,60},{24,64},{28,68},{32,7... | collective-permute-start | bytes 49160
  687.5 65.1 %all-to-all-start.6 = ((bf16[20,16,512]{2,1,0:T(8,128)(2,1)}), bf16[20,16,512]{2,1,0:T(8,128)(2,1)S(1)}, u32[]{:S(2)}, u32[]{:S(2)}) async-start(bf16[20,16,512]{2,1,0:T(8,128)(2,1)} %convert_element_type.109), calls=%async_computation.6 | async-start | bytes 655360 | tf_op jit(solution)/shard_map/all_to_all | solution.py:208
  694.6 68.9 %reduce-scatter.7.cloned.1.call-start = ((), (), s32[]{:S(2)}) async-start(), calls=%async_computation.10 | async-start | bytes 20480 | tf_op jit(solution)/shard_map/reduce_scatter | solution.py:234
  694.6 24.8 %collective-permute-start.44 = (f32[512,8]{0,1:T(8,128)S(1)}, f32[512,8]{0,1:T(8,128)S(1)}, u32[]{:S(2)}, u32[]{:S(2)}) collective-permute-start(f32[512,8]{0,1:T(8,128)S(1)} %get-tuple-element.51), channel_id=1, source_target_pairs={{0,36},{4,40},{8,44},{12,48},{16,52},{20,56},{24,60},{28,64},{32,6... | collective-permute-start | bytes 49160
  698.1 27.4 %collective-permute-start.43 = (f32[512,8]{0,1:T(8,128)S(1)}, f32[512,8]{0,1:T(8,128)S(1)}, u32[]{:S(2)}, u32[]{:S(2)}) collective-permute-start(f32[512,8]{0,1:T(8,128)S(1)} %get-tuple-element.51), channel_id=1, source_target_pairs={{0,32},{4,36},{8,40},{12,44},{16,48},{20,52},{24,56},{28,60},{32,6... | collective-permute-start | bytes 49160
  701.2 26.2 %collective-permute-start.42 = (f32[512,8]{0,1:T(8,128)S(1)}, f32[512,8]{0,1:T(8,128)S(1)}, u32[]{:S(2)}, u32[]{:S(2)}) collective-permute-start(f32[512,8]{0,1:T(8,128)S(1)} %get-tuple-element.51), channel_id=1, source_target_pairs={{0,28},{4,32},{8,36},{12,40},{16,44},{20,48},{24,52},{28,56},{32,6... | collective-permute-start | bytes 49160
  703.2 26.2 %collective-permute-start.41 = (f32[512,8]{0,1:T(8,128)S(1)}, f32[512,8]{0,1:T(8,128)}, u32[]{:S(2)}, u32[]{:S(2)}) collective-permute-start(f32[512,8]{0,1:T(8,128)S(1)} %get-tuple-element.51), channel_id=1, source_target_pairs={{0,24},{4,28},{8,32},{12,36},{16,40},{20,44},{24,48},{28,52},{32,5... | collective-permute-start | bytes 49160
  719.4 29.9 %collective-permute-start.3 = (f32[5,15,512]{2,1,0:T(8,128)S(1)}, f32[5,15,512]{2,1,0:T(8,128)S(1)}, u32[]{:S(2)}, u32[]{:S(2)}) collective-permute-start(f32[5,15,512]{2,1,0:T(8,128)S(1)} %copy-done.31), channel_id=1, source_target_pairs={{4,0},{8,4},{12,8},{16,12},{20,16},{24,20},{28,24},{32,28},{36,32}... | collective-permute-start | bytes 460808 | tf_op jit(solution)/shard_map/ppermute | solution.py:14
  734.8 58.3 %reduce-scatter.9.cloned.1.call-start = ((), (), s32[]{:S(2)}) async-start(), calls=%async_computation.11 | async-start | bytes 20480 | tf_op jit(solution)/shard_map/reduce_scatter | solution.py:235
  (150 other events, 3016.8 us)
Sparse Core Ops, SparseCore 0:
  734.9 28.4 reduce-scatter.6
  767.0 25.9 reduce-scatter.8
where the time goes:
time: 810 us; the launch traced here: 800 us
  blocking collectives  317 us (39%)
  starting transfers between devices  283 us (35%)
  local copies, waits for them, and re-layouts  64.7 us (8%)
  waiting for transfers between devices  52.9 us (7%)
  matrix products  37.2 us (5%)
  other arithmetic  27.2 us (3%)
  between operations  17.5 us (2%)
    unnamed x1, blocking collectives  269 us
    unnamed x64, starting transfers between devices  206 us
    unnamed x223, local copies, waits for them, and re-layouts  35.6 us
    all_gather x1, blocking collectives, per_device(): lax.all_gather(out_time, 'series', axis=0, tiled=True)  30.3 us
    reduce_scatter x1, waiting for transfers between devices, per_device(): lax.psum_scatter(partial_sums[1], 'series', scatter_dimension=0, tiled=True)  29.6 us
    ppermute x4, starting transfers between devices, passed_along(): lax.ppermute(value, axis, [(source, source + steps) for source in range(l...  29.5 us
    all_gather x1, blocking collectives, per_device(): lax.all_gather(out_group, 'series', axis=0, tiled=True)  17.7 us
  transfers between devices with their start and end apart: 78, of which 9 were waited for; matrix products, arithmetic and copies ran while one was open for 49% of the time, Pallas kernels for 0%

commit v1 on v0

--- a/solution.py
+++ b/solution.py
@@ -6,6 +6,9 @@
 HEAD_DIM = 64
 BAND = 16
 masked_score = -1e30
+store_entries = lambda z, across, array_dim: jnp.concatenate(
+    lax.all_to_all(jnp.stack(lax.axis_size(across) * [z], axis=0), across, 0, 0), axis=array_dim
+)
 
 
 def passed_along(value, axis, steps):
@@ -157,7 +160,7 @@
     border_rows = BAND - 1
     w_time, w_group = (
         lax.all_gather(out_time, "series", axis=0, tiled=True),
-        lax.all_gather(out_group, "series", axis=0, tiled=True),
+        store_entries(out_group, "series", array_dim=0),
     )
     cot_flat = cotangent.reshape(-1, cotangent.shape[2])
 

time: 810 us -> 815 us (level)
  blocking collectives: 317 us -> 299 us
  waiting for transfers between devices: 52.9 us -> 61.2 us
    all_gather x1 -> x0, blocking collectives: 17.7 us -> none  [per_device(): lax.all_gather(out_group, 'series', axis=0, tiled=True)]
    unnamed x223 -> x203, local copies, waits for them, and re-layouts: 35.6 us -> 36.4 us
  transfers between devices with their start and end apart: 78 -> 79, of which waited for: 9 -> 8; matrix products, arithmetic and copies ran while one was open for 49% -> 49% of each run, Pallas kernels for 0% -> 0%
where the time goes in v1:
time: 815 us; the launch traced here: 802 us
  blocking collectives  299 us (37%)
  starting transfers between devices  290 us (36%)
  local copies, waits for them, and re-layouts  67.6 us (8%)
  waiting for transfers between devices  61.2 us (8%)
  matrix products  40.5 us (5%)
  other arithmetic  26.9 us (3%)
  between operations  17.3 us (2%)
    unnamed x1, blocking collectives  270 us
    unnamed x64, starting transfers between devices  208 us
    unnamed x203, local copies, waits for them, and re-layouts  36.4 us
    reduce_scatter x1, waiting for transfers between devices, per_device(): lax.psum_scatter(partial_sums[1], 'series', scatter_dimension=0, tiled=True)  29.6 us
    all_gather x1, blocking collectives, per_device(): lax.all_gather(out_time, 'series', axis=0, tiled=True)  29.3 us
    ppermute x4, starting transfers between devices, passed_along(): lax.ppermute(value, axis, [(source, source + steps) for source in range(l...  28.3 us
  transfers between devices with their start and end apart: 79, of which 8 were waited for; matrix products, arithmetic and copies ran while one was open for 49% of the time, Pallas kernels for 0%

profile of v1, /device:TPU:2, one launch (start us, length us, event | category | flops | bytes accessed | tf_op | source)
XLA Modules:
  0.0 802.1 jit_solution(10565482842723886639)
XLA Ops:
  12.3 19.1 %collective-permute-start.1 = (bf16[5,15,512]{2,1,0:T(8,128)(2,1)}, bf16[5,15,512]{2,1,0:T(8,128)(2,1)}, u32[]{:S(2)}, u32[]{:S(2)}) collective-permute-start(bf16[5,15,512]{2,1,0:T(8,128)(2,1)} %slice.19), channel_id=1, source_target_pairs={{0,4},{4,8},{8,12},{12,16},{16,20},{20,24},{24,28},{28,32},{32,36}... | collective-permute-start | bytes 230408 | tf_op jit(solution)/shard_map/ppermute | solution.py:17
  33.3 8.7 %all-to-all-start.4 = ((bf16[5,64,512]{2,0,1:T(8,128)(2,1)}), bf16[5,64,512]{2,0,1:T(8,128)(2,1)S(1)}, u32[]{:S(2)}, u32[]{:S(2)}) async-start(bf16[5,64,512]{2,0,1:T(8,128)(2,1)} %copy.160), calls=%async_computation.4 | async-start | bytes 1048576 | tf_op jit(solution)/shard_map/all_to_all | solution.py:203
  43.2 29.3 %all_gather.3 = bf16[512,768]{1,0:T(8,128)(2,1)S(1)} all-gather(bf16[128,768]{1,0:T(8,128)(2,1)S(1)} %copy-done.23), channel_id=1, replica_groups=mesh['tm'=128,'series'=4] {'series'}, dimensions={0}, use_global_device_ids=true | all-gather | bytes 983040 | tf_op jit(solution)/shard_map/all_gather | solution.py:162
  72.5 4.7 all-to-all-start.1
  82.6 8.3 %all-to-all-done.1 = bf16[5,64,512]{2,0,1:T(8,128)(2,1)S(1)} async-done(((bf16[5,64,512]{2,0,1:T(8,128)(2,1)}), bf16[5,64,512]{2,0,1:T(8,128)(2,1)S(1)}, u32[]{:S(2)}, u32[]{:S(2)}) %all-to-all-start.1) | async-done | bytes 327712 | tf_op jit(solution)/shard_map/all_to_all | solution.py:202
  102.0 4.2 all-to-all-done
  116.9 6.0 all-to-all-start.8
  127.2 5.4 all-to-all-done.8
  147.9 7.3 convolution_convert_fusion.5
  161.6 7.2 all-to-all-start.3
  168.8 269.5 %fusion.52 = (f32[512,8]{0,1:T(8,128)S(1)}, f32[512,8]{0,1:T(8,128)S(1)}) fusion(f32[512,768]{0,1:T(8,128)} %bitcast_multiply_fusion, f32[512,768]{0,1:T(8,128)} %convolution_multiply_fusion), kind=kCustom, calls=%all-reduce-scatter.2 | all-reduce-scatter fusion | flops 1048577 | bytes 3180544
  439.6 12.3 %collective-permute-start.33 = (f32[512,8]{0,1:T(8,128)S(1)}, f32[512,8]{0,1:T(8,128)S(1)}, u32[]{:S(2)}, u32[]{:S(2)}) collective-permute-start(f32[512,8]{0,1:T(8,128)S(1)} %get-tuple-element.50), channel_id=1, source_target_pairs={{0,120},{4,124},{8,128},{12,132},{16,136},{20,140},{24,144},{28,14... | collective-permute-start | bytes 49160
  451.9 7.8 collective-permute-start.32
  462.5 18.1 %collective-permute-start.31 = (f32[512,8]{0,1:T(8,128)S(1)}, f32[512,8]{0,1:T(8,128)S(1)}, u32[]{:S(2)}, u32[]{:S(2)}) collective-permute-start(f32[512,8]{0,1:T(8,128)S(1)} %get-tuple-element.50), channel_id=1, source_target_pairs={{0,112},{4,116},{8,120},{12,124},{16,128},{20,132},{24,136},{28,14... | collective-permute-start | bytes 49160
  480.6 10.9 %collective-permute-start.30 = (f32[512,8]{0,1:T(8,128)S(1)}, f32[512,8]{0,1:T(8,128)S(1)}, u32[]{:S(2)}, u32[]{:S(2)}) collective-permute-start(f32[512,8]{0,1:T(8,128)S(1)} %get-tuple-element.50), channel_id=1, source_target_pairs={{0,108},{4,112},{8,116},{12,120},{16,124},{20,128},{24,132},{28,13... | collective-permute-start | bytes 49160
  491.5 17.6 %collective-permute-start.29 = (f32[512,8]{0,1:T(8,128)S(1)}, f32[512,8]{0,1:T(8,128)S(1)}, u32[]{:S(2)}, u32[]{:S(2)}) collective-permute-start(f32[512,8]{0,1:T(8,128)S(1)} %get-tuple-element.50), channel_id=1, source_target_pairs={{0,104},{4,108},{8,112},{12,116},{16,120},{20,124},{24,128},{28,13... | collective-permute-start | bytes 49160
  520.1 4.5 collective-permute-start.22
  555.9 4.2 collective-permute-start.11
  572.4 14.9 %fusion.10 = f32[16,8,20,20]{3,1,2,0:T(8,128)} fusion(bf16[16,8,20,20]{3,1,2,0:T(8,128)(2,1)S(1)} %copy.214, f32[16,8,20,20]{3,1,2,0:T(8,128)S(1)} %copy-done.8, f32[16,8,20]{1,2,0:T(8,128)S(1)} %copy-done.19), kind=kOutput, calls=%fused_computation.14 | output fusion | flops 412179 | bytes 522240 | tf_op jit(solution)/shard_map/sub | solution.py:29
  606.0 5.1 all-to-all-start.5
  620.5 4.2 convolution_convert_fusion.4
  648.9 6.9 all-to-all-start.6
  655.9 7.4 fusion.45
  692.0 4.4 collective-permute-start.43
  698.4 4.3 collective-permute-start.41
  704.6 7.2 all-to-all-start.7
  712.8 9.6 %concatenate.16 = f32[512,262]{0,1:T(8,128)S(1)} concatenate(f32[512,6]{0,1:T(8,128)S(1)} %copy-done.33, f32[512,8]{0,1:T(8,128)S(1)} %collective-permute-done.34, f32[512,8]{0,1:T(8,128)S(1)} %copy-done.29, f32[512,8]{0,1:T(8,128)S(1)} %copy-done.31, f32[512,8]{0,1:T(8,128)S(1)} %copy-done.35, f32[512,8]{0,1:T(8,128)S(1)} %copy-done.37, f32[512,8]{0,1:T(8,128)S(1)} %copy-done.39, ...), dimensions={1} | concatenate | bytes 1073152
  722.4 5.4 collective-permute-start.3
  734.0 4.4 collective-permute-start.36
  743.4 8.1 %concatenate.17 = f32[512,262]{0,1:T(8,128)S(1)} concatenate(f32[512,6]{0,1:T(8,128)S(1)} %collective-permute-done.67, f32[512,8]{0,1:T(8,128)S(1)} %copy-done.65, f32[512,8]{0,1:T(8,128)S(1)} %copy-done.67, f32[512,8]{0,1:T(8,128)S(1)} %copy-done.75, f32[512,8]{0,1:T(8,128)S(1)} %copy-done.79, f32[512,8]{0,1:T(8,128)S(1)} %copy-done.81, f32[512,8]{0,1:T(8,128)S(1)} %copy-done.83, ...), dimensions={1} | concatenate | bytes 1073152
  756.2 9.3 %reduce-scatter.7.cloned.1.call-done = f32[128,6]{0,1:T(8,128)} async-done(((f32[512,6]{0,1:T(8,128)}), f32[128,6]{0,1:T(8,128)}) %reduce-scatter.7.cloned.1.call-update) | async-done | bytes 3088 | tf_op jit(solution)/shard_map/reduce_scatter | solution.py:237
  765.5 29.6 %reduce-scatter.9.cloned.1.call-done = f32[128,6]{0,1:T(8,128)} async-done(((f32[512,6]{0,1:T(8,128)}), f32[128,6]{0,1:T(8,128)}) %reduce-scatter.9.cloned.1.call-update) | async-done | bytes 3088 | tf_op jit(solution)/shard_map/reduce_scatter | solution.py:238
  (398 shorter events, 219.0 us)
Async XLA Ops:
  8.8 85.5 %collective-permute-start = (bf16[5,15,512]{2,1,0:T(8,128)(2,1)}, bf16[5,15,512]{2,1,0:T(8,128)(2,1)}, u32[]{:S(2)}, u32[]{:S(2)}) collective-permute-start(bf16[5,15,512]{2,1,0:T(8,128)(2,1)} %slice.18), channel_id=1, source_target_pairs={{0,4},{4,8},{8,12},{12,16},{16,20},{20,24},{24,28},{28,32},{32,36}... | collective-permute-start | bytes 230408 | tf_op jit(solution)/shard_map/ppermute | solution.py:17
  12.3 84.3 %collective-permute-start.1 = (bf16[5,15,512]{2,1,0:T(8,128)(2,1)}, bf16[5,15,512]{2,1,0:T(8,128)(2,1)}, u32[]{:S(2)}, u32[]{:S(2)}) collective-permute-start(bf16[5,15,512]{2,1,0:T(8,128)(2,1)} %slice.19), channel_id=1, source_target_pairs={{0,4},{4,8},{8,12},{12,16},{16,20},{20,24},{24,28},{28,32},{32,36}... | collective-permute-start | bytes 230408 | tf_op jit(solution)/shard_map/ppermute | solution.py:17
  33.3 39.2 %all-to-all-start.4 = ((bf16[5,64,512]{2,0,1:T(8,128)(2,1)}), bf16[5,64,512]{2,0,1:T(8,128)(2,1)S(1)}, u32[]{:S(2)}, u32[]{:S(2)}) async-start(bf16[5,64,512]{2,0,1:T(8,128)(2,1)} %copy.160), calls=%async_computation.4 | async-start | bytes 1048576 | tf_op jit(solution)/shard_map/all_to_all | solution.py:203
  133.6 26.5 %all-to-all-start.2 = ((bf16[4,128,768]{2,1,0:T(8,128)(2,1)}), bf16[4,128,768]{2,1,0:T(8,128)(2,1)S(1)}, u32[]{:S(2)}, u32[]{:S(2)}) async-start(bf16[4,128,768]{2,1,0:T(8,128)(2,1)} %stack.2), calls=%async_computation.2 | async-start | bytes 1572864 | tf_op jit(solution)/shard_map/all_to_all | solution.py:10
  146.0 315.1 %collective-permute-start.2 = (f32[5,15,512]{2,1,0:T(8,128)}, f32[5,15,512]{2,1,0:T(8,128)S(1)}, u32[]{:S(2)}, u32[]{:S(2)}) collective-permute-start(f32[5,15,512]{2,1,0:T(8,128)} %copy.186), channel_id=1, source_target_pairs={{4,0},{8,4},{12,8},{16,12},{20,16},{24,20},{28,24},{32,28},{36,32}... | collective-permute-start | bytes 460808 | tf_op jit(solution)/shard_map/ppermute | solution.py:17
  161.6 378.1 %all-to-all-start.3 = ((bf16[5,64,512]{2,0,1:T(8,128)(2,1)}), bf16[5,64,512]{2,0,1:T(8,128)(2,1)S(1)}, u32[]{:S(2)}, u32[]{:S(2)}) async-start(bf16[5,64,512]{2,0,1:T(8,128)(2,1)} %copy.157), calls=%async_computation.3 | async-start | bytes 1048576 | tf_op jit(solution)/shard_map/all_to_all | solution.py:204
  438.3 53.2 %collective-permute-start.34 = (f32[512,8]{0,1:T(8,128)S(1)}, f32[512,8]{0,1:T(8,128)S(1)}, u32[]{:S(2)}, u32[]{:S(2)}) collective-permute-start(f32[512,8]{0,1:T(8,128)S(1)} %get-tuple-element.50), channel_id=1, source_target_pairs={{0,124},{4,128},{8,132},{12,136},{16,140},{20,144},{24,148},{28,15... | collective-permute-start | bytes 49160
  439.6 69.6 %collective-permute-start.33 = (f32[512,8]{0,1:T(8,128)S(1)}, f32[512,8]{0,1:T(8,128)S(1)}, u32[]{:S(2)}, u32[]{:S(2)}) collective-permute-start(f32[512,8]{0,1:T(8,128)S(1)} %get-tuple-element.50), channel_id=1, source_target_pairs={{0,120},{4,124},{8,128},{12,132},{16,136},{20,140},{24,144},{28,14... | collective-permute-start | bytes 49160
  451.9 59.2 %collective-permute-start.32 = (f32[512,8]{0,1:T(8,128)S(1)}, f32[512,8]{0,1:T(8,128)S(1)}, u32[]{:S(2)}, u32[]{:S(2)}) collective-permute-start(f32[512,8]{0,1:T(8,128)S(1)} %get-tuple-element.50), channel_id=1, source_target_pairs={{0,116},{4,120},{8,124},{12,128},{16,132},{20,136},{24,140},{28,14... | collective-permute-start | bytes 49160
  462.5 51.7 %collective-permute-start.31 = (f32[512,8]{0,1:T(8,128)S(1)}, f32[512,8]{0,1:T(8,128)S(1)}, u32[]{:S(2)}, u32[]{:S(2)}) collective-permute-start(f32[512,8]{0,1:T(8,128)S(1)} %get-tuple-element.50), channel_id=1, source_target_pairs={{0,112},{4,116},{8,120},{12,124},{16,128},{20,132},{24,136},{28,14... | collective-permute-start | bytes 49160
  480.6 35.0 %collective-permute-start.30 = (f32[512,8]{0,1:T(8,128)S(1)}, f32[512,8]{0,1:T(8,128)S(1)}, u32[]{:S(2)}, u32[]{:S(2)}) collective-permute-start(f32[512,8]{0,1:T(8,128)S(1)} %get-tuple-element.50), channel_id=1, source_target_pairs={{0,108},{4,112},{8,116},{12,120},{16,124},{20,128},{24,132},{28,13... | collective-permute-start | bytes 49160
  555.9 33.6 %collective-permute-start.11 = (f32[512,8]{0,1:T(8,128)S(1)}, f32[512,8]{0,1:T(8,128)S(1)}, u32[]{:S(2)}, u32[]{:S(2)}) collective-permute-start(f32[512,8]{0,1:T(8,128)S(1)} %get-tuple-element.50), channel_id=1, source_target_pairs={{0,32},{4,36},{8,40},{12,44},{16,48},{20,52},{24,56},{28,60},{32,6... | collective-permute-start | bytes 49160
  560.1 32.9 %collective-permute-start.10 = (f32[512,8]{0,1:T(8,128)S(1)}, f32[512,8]{0,1:T(8,128)S(1)}, u32[]{:S(2)}, u32[]{:S(2)}) collective-permute-start(f32[512,8]{0,1:T(8,128)S(1)} %get-tuple-element.50), channel_id=1, source_target_pairs={{0,28},{4,32},{8,36},{12,40},{16,44},{20,48},{24,52},{28,56},{32,6... | collective-permute-start | bytes 49160
  562.1 32.9 %collective-permute-start.9 = (f32[512,8]{0,1:T(8,128)S(1)}, f32[512,8]{0,1:T(8,128)S(1)}, u32[]{:S(2)}, u32[]{:S(2)}) collective-permute-start(f32[512,8]{0,1:T(8,128)S(1)} %get-tuple-element.50), channel_id=1, source_target_pairs={{0,24},{4,28},{8,32},{12,36},{16,40},{20,44},{24,48},{28,52},{32,5... | collective-permute-start | bytes 49160
  566.1 31.1 %collective-permute-start.8 = (f32[512,8]{0,1:T(8,128)S(1)}, f32[512,8]{0,1:T(8,128)S(1)}, u32[]{:S(2)}, u32[]{:S(2)}) collective-permute-start(f32[512,8]{0,1:T(8,128)S(1)} %get-tuple-element.50), channel_id=1, source_target_pairs={{0,20},{4,24},{8,28},{12,32},{16,36},{20,40},{24,44},{28,48},{32,5... | collective-permute-start | bytes 49160
  570.0 28.5 %collective-permute-start.7 = (f32[512,8]{0,1:T(8,128)S(1)}, f32[512,8]{0,1:T(8,128)}, u32[]{:S(2)}, u32[]{:S(2)}) collective-permute-start(f32[512,8]{0,1:T(8,128)S(1)} %get-tuple-element.50), channel_id=1, source_target_pairs={{0,16},{4,20},{8,24},{12,28},{16,32},{20,36},{24,40},{28,44},{32,4... | collective-permute-start | bytes 49160
  606.0 42.9 %all-to-all-start.5 = ((bf16[20,16,512]{2,1,0:T(8,128)(2,1)}), bf16[20,16,512]{2,1,0:T(8,128)(2,1)}, u32[]{:S(2)}, u32[]{:S(2)}) async-start(bf16[20,16,512]{2,1,0:T(8,128)(2,1)} %convert_element_type.102), calls=%async_computation.5 | async-start | bytes 655360 | tf_op jit(solution)/shard_map/all_to_all | solution.py:209
  638.1 36.5 %collective-permute-start.54 = (f32[512,8]{0,1:T(8,128)S(1)}, f32[512,8]{0,1:T(8,128)}, u32[]{:S(2)}, u32[]{:S(2)}) collective-permute-start(f32[512,8]{0,1:T(8,128)S(1)} %get-tuple-element.51), channel_id=1, source_target_pairs={{0,76},{4,80},{8,84},{12,88},{16,92},{20,96},{24,100},{28,104},{32... | collective-permute-start | bytes 49160
  640.0 36.6 %collective-permute-start.53 = (f32[512,8]{0,1:T(8,128)S(1)}, f32[512,8]{0,1:T(8,128)}, u32[]{:S(2)}, u32[]{:S(2)}) collective-permute-start(f32[512,8]{0,1:T(8,128)S(1)} %get-tuple-element.51), channel_id=1, source_target_pairs={{0,72},{4,76},{8,80},{12,84},{16,88},{20,92},{24,96},{28,100},{32,... | collective-permute-start | bytes 49160
  642.2 36.3 %collective-permute-start.52 = (f32[512,8]{0,1:T(8,128)S(1)}, f32[512,8]{0,1:T(8,128)}, u32[]{:S(2)}, u32[]{:S(2)}) collective-permute-start(f32[512,8]{0,1:T(8,128)S(1)} %get-tuple-element.51), channel_id=1, source_target_pairs={{0,68},{4,72},{8,76},{12,80},{16,84},{20,88},{24,92},{28,96},{32,1... | collective-permute-start | bytes 49160
  644.0 36.5 %collective-permute-start.51 = (f32[512,8]{0,1:T(8,128)S(1)}, f32[512,8]{0,1:T(8,128)}, u32[]{:S(2)}, u32[]{:S(2)}) collective-permute-start(f32[512,8]{0,1:T(8,128)S(1)} %get-tuple-element.51), channel_id=1, source_target_pairs={{0,64},{4,68},{8,72},{12,76},{16,80},{20,84},{24,88},{28,92},{32,9... | collective-permute-start | bytes 49160
  646.0 36.8 %collective-permute-start.50 = (f32[512,8]{0,1:T(8,128)S(1)}, f32[512,8]{0,1:T(8,128)}, u32[]{:S(2)}, u32[]{:S(2)}) collective-permute-start(f32[512,8]{0,1:T(8,128)S(1)} %get-tuple-element.51), channel_id=1, source_target_pairs={{0,60},{4,64},{8,68},{12,72},{16,76},{20,80},{24,84},{28,88},{32,9... | collective-permute-start | bytes 49160
  648.9 55.7 %all-to-all-start.6 = ((bf16[20,16,512]{2,1,0:T(8,128)(2,1)}), bf16[20,16,512]{2,1,0:T(8,128)(2,1)S(1)}, u32[]{:S(2)}, u32[]{:S(2)}) async-start(bf16[20,16,512]{2,1,0:T(8,128)(2,1)} %convert_element_type.105), calls=%async_computation.6 | async-start | bytes 655360 | tf_op jit(solution)/shard_map/all_to_all | solution.py:210
  688.6 33.8 %collective-permute-start.44 = (f32[512,8]{0,1:T(8,128)S(1)}, f32[512,8]{0,1:T(8,128)S(1)}, u32[]{:S(2)}, u32[]{:S(2)}) collective-permute-start(f32[512,8]{0,1:T(8,128)S(1)} %get-tuple-element.51), channel_id=1, source_target_pairs={{0,36},{4,40},{8,44},{12,48},{16,52},{20,56},{24,60},{28,64},{32,6... | collective-permute-start | bytes 49160
  692.0 35.8 %collective-permute-start.43 = (f32[512,8]{0,1:T(8,128)S(1)}, f32[512,8]{0,1:T(8,128)S(1)}, u32[]{:S(2)}, u32[]{:S(2)}) collective-permute-start(f32[512,8]{0,1:T(8,128)S(1)} %get-tuple-element.51), channel_id=1, source_target_pairs={{0,32},{4,36},{8,40},{12,44},{16,48},{20,52},{24,56},{28,60},{32,6... | collective-permute-start | bytes 49160
  696.4 33.3 %collective-permute-start.42 = (f32[512,8]{0,1:T(8,128)S(1)}, f32[512,8]{0,1:T(8,128)S(1)}, u32[]{:S(2)}, u32[]{:S(2)}) collective-permute-start(f32[512,8]{0,1:T(8,128)S(1)} %get-tuple-element.51), channel_id=1, source_target_pairs={{0,28},{4,32},{8,36},{12,40},{16,44},{20,48},{24,52},{28,56},{32,6... | collective-permute-start | bytes 49160
  698.4 33.5 %collective-permute-start.41 = (f32[512,8]{0,1:T(8,128)S(1)}, f32[512,8]{0,1:T(8,128)S(1)}, u32[]{:S(2)}, u32[]{:S(2)}) collective-permute-start(f32[512,8]{0,1:T(8,128)S(1)} %get-tuple-element.51), channel_id=1, source_target_pairs={{0,24},{4,28},{8,32},{12,36},{16,40},{20,44},{24,48},{28,52},{32,5... | collective-permute-start | bytes 49160
  702.7 31.3 %collective-permute-start.40 = (f32[512,8]{0,1:T(8,128)S(1)}, f32[512,8]{0,1:T(8,128)S(1)}, u32[]{:S(2)}, u32[]{:S(2)}) collective-permute-start(f32[512,8]{0,1:T(8,128)S(1)} %get-tuple-element.51), channel_id=1, source_target_pairs={{0,20},{4,24},{8,28},{12,32},{16,36},{20,40},{24,44},{28,48},{32,5... | collective-permute-start | bytes 49160
  704.6 50.8 %all-to-all-start.7 = ((bf16[20,16,512]{2,1,0:T(8,128)(2,1)}), bf16[20,16,512]{2,1,0:T(8,128)(2,1)S(1)}, u32[]{:S(2)}, u32[]{:S(2)}) async-start(bf16[20,16,512]{2,1,0:T(8,128)(2,1)} %convert_element_type.109), calls=%async_computation.7 | async-start | bytes 655360 | tf_op jit(solution)/shard_map/all_to_all | solution.py:211
  711.8 53.6 %reduce-scatter.7.cloned.1.call-start = ((), (), s32[]{:S(2)}) async-start(), calls=%async_computation.11 | async-start | bytes 20480 | tf_op jit(solution)/shard_map/reduce_scatter | solution.py:237
  722.4 29.7 %collective-permute-start.3 = (f32[5,15,512]{2,1,0:T(8,128)S(1)}, f32[5,15,512]{2,1,0:T(8,128)S(1)}, u32[]{:S(2)}, u32[]{:S(2)}) collective-permute-start(f32[5,15,512]{2,1,0:T(8,128)S(1)} %copy-done.27), channel_id=1, source_target_pairs={{4,0},{8,4},{12,8},{16,12},{20,16},{24,20},{28,24},{32,28},{36,32}... | collective-permute-start | bytes 460808 | tf_op jit(solution)/shard_map/ppermute | solution.py:17
  739.1 56.0 %reduce-scatter.9.cloned.1.call-start = ((), (), s32[]{:S(2)}) async-start(), calls=%async_computation.12 | async-start | bytes 20480 | tf_op jit(solution)/shard_map/reduce_scatter | solution.py:238
  (141 other events, 2814.9 us)
Sparse Core Ops, SparseCore 0:
  739.2 26.2 reduce-scatter.6
  769.0 25.9 reduce-scatter.8
